TPU v7x, 32 devices: a whole 2x2x4 slice. The times are simulated.
32 devices in a mesh: az: 8 (over y, x, core), rg: 4 (over z).
Axes of the slice: x: 2, y: 2, z: 4, core: 2. Of those that a mesh axis runs over, the one named last changes fastest.
Arguments:
- raw: bfloat16 [2, 4096, 8192], P(None, 'az', 'rg'), may hold values from -6 to 6
- chirp: bfloat16 [2, 256], replicated, may hold values from -0.25 to 0.25
- az_ref: bfloat16 [2, 64, 512], replicated, may hold values from -0.1875 to 0.1875
- set_index: int32 [8192], P('rg'), may hold values from 0 to 63, as said below
Outputs:
- focused: bfloat16 [2, 4096, 8192], P(None, 'az', 'rg')
Inputs may be any that keep to these rules, and one draw needn't show every extreme that they name: `set_index`: range columns come in aligned runs of 256 that share one set index.
All inputs are finite; a program needn't handle non-finite values.
Results may differ from a plain program's by a relative error of at most 0.0049.
Values may be sent and summed in bfloat16 or wider, within the bound.
A program may use at most 64 MiB of HBM per device.

v0:
```python
import jax
import jax.numpy as jnp
from jax import lax
from jax.sharding import PartitionSpec as P


def passed_along(block, axis, distance):
    devices = range(lax.axis_size(axis))
    route = [(i - distance, i) for i in devices if i - distance in devices]
    return lax.ppermute(block, axis, route)


def toeplitz(ref_taps, span_out):
    tap_count = ref_taps.shape[1]
    period = span_out + tap_count + 1
    padded = jnp.concatenate([ref_taps, jnp.zeros((2, span_out + 1), ref_taps.dtype)], axis=1)
    tiled = jnp.tile(padded, (1, span_out))[:, : span_out * (period - 1)]
    return tiled.reshape(2 * span_out, period - 1)


def range_compress(window, weights, block_size, count):
    lines = window.shape[1]
    span = weights.shape[1]
    output = jnp.zeros((2, lines, block_size * count), jnp.bfloat16)

    def range_one_block(block_index, current):
        segment = lax.dynamic_slice_in_dim(window, block_index * block_size, span, axis=2)
        product = lax.dot_general(
            segment.reshape(2 * lines, span),
            weights,
            (((1,), (1,)), ((), ())),
            preferred_element_type=jnp.float32,
        )
        real_part = product[:lines, :block_size] + product[lines:, block_size:]
        imag_part = product[lines:, :block_size] - product[:lines, block_size:]
        piece = jnp.stack([real_part, imag_part]).astype(jnp.bfloat16)
        return lax.dynamic_update_slice_in_dim(current, piece, block_index * block_size, axis=2)

    return lax.fori_loop(0, count, range_one_block, output)


def azimuth_compress(window, weights, lines, block_size):
    columns = window.shape[2]
    span = weights.shape[1]
    output = jnp.zeros((2, lines, columns), jnp.bfloat16)

    def azimuth_one_block(block_index, current):
        segment = lax.dynamic_slice_in_dim(window, block_index * block_size, span, axis=1)
        real_prod = jnp.dot(weights, segment[0], preferred_element_type=jnp.float32)
        imag_prod = jnp.dot(weights, segment[1], preferred_element_type=jnp.float32)
        real_part = real_prod[:block_size] + imag_prod[block_size:]
        imag_part = imag_prod[:block_size] - real_prod[block_size:]
        piece = jnp.stack([real_part, imag_part]).astype(jnp.bfloat16)
        return lax.dynamic_update_slice_in_dim(current, piece, block_index * block_size, axis=1)

    return lax.fori_loop(0, lines // block_size, azimuth_one_block, output)


def local(raw, chirp, az_ref, set_index):
    lines = raw.shape[1]
    columns = raw.shape[2]
    range_taps = chirp.shape[1]
    azimuth_taps = az_ref.shape[2]
    next_columns = passed_along(raw[:, :, :range_taps], "rg", -1)
    window = jnp.concatenate([raw, next_columns], axis=2)
    block_size = min(512, columns)
    compressed = range_compress(
        window, toeplitz(chirp, block_size), block_size, columns // block_size
    )
    group_count = lax.axis_size("az")
    group_width = columns // group_count
    position = lax.axis_index("az") * group_width
    chosen = lax.dynamic_index_in_dim(set_index, position, 0, keepdims=False)
    ref_taps = lax.dynamic_index_in_dim(az_ref, chosen, 1, keepdims=False)
    all_lines = lines * group_count
    line_block = min(512, all_lines)
    weights = toeplitz(ref_taps, line_block)
    grouped = compressed.reshape(2, lines, group_count, group_width)
    segment = lax.all_to_all(grouped, "az", split_axis=2, concat_axis=1, tiled=True)
    width = segment.shape[3]
    merged = segment.reshape(2, segment.shape[1], width)
    padded = jnp.concatenate([merged, jnp.zeros((2, azimuth_taps, width), merged.dtype)], axis=1)
    result = azimuth_compress(padded, weights, merged.shape[1], line_block)
    turned = result.reshape(2, merged.shape[1], 1, width)
    returned = lax.all_to_all(turned, "az", split_axis=1, concat_axis=2, tiled=True)
    focused = returned.reshape(2, lines, columns)
    return focused


def solution(mesh):
    in_specs = (P(None, "az", "rg"), P(), P(), P("rg"))
    out_specs = P(None, "az", "rg")
    return jax.shard_map(local, mesh=mesh, in_specs=in_specs, out_specs=out_specs, check_vma=False)
```

profile of v0, /device:TPU:1, one launch (start us, length us, event | category | flops | bytes accessed | tf_op | source)
XLA Modules:
  0.0 230.7 jit_solution(6144009068772396893)
XLA Ops:
  0.0 1.9 slice.79
  1.9 1.3 collective-permute-start
  3.2 0.7 concatenate.13
  4.0 2.7 %reshape.41 = bf16[787456]{0:T(1024)(128)(2,1)S(1)} reshape(bf16[2,512,769]{2,1,0:T(8,128)(2,1)S(1)} %tile.8) | data formatting | bytes 3149824
  7.1 1.1 slice.90
  8.3 2.2 reshape.35
  10.4 7.4 %collective-permute-done = bf16[2,512,256]{2,1,0:T(8,128)(2,1)} collective-permute-done((bf16[2,512,256]{2,1,0:T(8,128)(2,1)}, bf16[2,512,256]{2,1,0:T(8,128)(2,1)}, u32[]{:S(2)}, u32[]{:S(2)}) %collective-permute-start) | collective-permute-done | bytes 524320 | tf_op jit(solution)/shard_map/ppermute | solution.py:10
  17.9 4.9 %pad_maximum_fusion.2 = bf16[2,512,2304]{2,1,0:T(8,128)(2,1)} fusion(bf16[2,512,256]{2,1,0:T(8,128)(2,1)} %collective-permute-done, bf16[2,512,2048]{2,1,0:T(8,128)(2,1)} %param.8), kind=kLoop, calls=%fused_computation.23 | loop fusion | flops 9437184 | bytes 9437184 | tf_op jit(solution)/shard_map/concatenate | solution.py:65
  22.8 2.3 broadcast_in_dim.8.clone
  25.1 27.3 %while.26 = (s32[]{:T(128)}, bf16[2,512,2048]{1,2,0:T(8,128)(2,1)}, bf16[2,512,2304]{2,1,0:T(8,128)(2,1)}, bf16[1024,768]{1,0:T(8,128)(2,1)}, s32[]{:T(128)}, /*index=5*/s32[]{:T(128)}, s32[]{:T(128)}, s32[]{:T(128)}, s32[]{:T(128)}) while((s32[]{:T(128)}, bf16[2,512,2048]{1,2,0:T(8,128)(2,1)}, bf16[2,512,2304]{2,1,0:T(8,128)(2,1)}, ...), condition=%wide.region_1.0_spmd, body=%wide.region_0.0_spmd.sunk | while | flops 1612185600 | bytes 22020268 | solution.py:39
  25.1 1.5 constant_dynamic-slice_fusion.3
  26.6 3.2 %fusion.24 = f32[1024,1024]{1,0:T(8,128)S(1)} fusion(bf16[1024,768]{1,0:T(8,128)(2,1)S(1)} %bitcast.63, bf16[1024,768]{1,0:T(8,128)(2,1)} %get-tuple-element.264), kind=kOutput, calls=%fused_computation.26.clone.1 | convolution fusion | flops 1610612736 | bytes 7340032 | tf_op jit(solution)/shard_map/while/body/eval_jaxpr/dot_general | solution.py:28
  30.3 0.5 copy.28
  30.8 1.0 constant_dynamic-update-slice_fusion.4
  31.9 1.5 constant_dynamic-slice_fusion.3
  33.4 3.2 %fusion.24 = f32[1024,1024]{1,0:T(8,128)S(1)} fusion(bf16[1024,768]{1,0:T(8,128)(2,1)S(1)} %bitcast.63, bf16[1024,768]{1,0:T(8,128)(2,1)} %get-tuple-element.264), kind=kOutput, calls=%fused_computation.26.clone.1 | convolution fusion | flops 1610612736 | bytes 7340032 | tf_op jit(solution)/shard_map/while/body/eval_jaxpr/dot_general | solution.py:28
  37.1 0.5 copy.28
  37.7 1.0 constant_dynamic-update-slice_fusion.4
  38.7 1.5 constant_dynamic-slice_fusion.3
  40.2 3.2 %fusion.24 = f32[1024,1024]{1,0:T(8,128)S(1)} fusion(bf16[1024,768]{1,0:T(8,128)(2,1)S(1)} %bitcast.63, bf16[1024,768]{1,0:T(8,128)(2,1)} %get-tuple-element.264), kind=kOutput, calls=%fused_computation.26.clone.1 | convolution fusion | flops 1610612736 | bytes 7340032 | tf_op jit(solution)/shard_map/while/body/eval_jaxpr/dot_general | solution.py:28
  43.9 0.5 copy.28
  44.5 1.0 constant_dynamic-update-slice_fusion.4
  45.5 1.5 constant_dynamic-slice_fusion.3
  47.0 3.2 %fusion.24 = f32[1024,1024]{1,0:T(8,128)S(1)} fusion(bf16[1024,768]{1,0:T(8,128)(2,1)S(1)} %bitcast.63, bf16[1024,768]{1,0:T(8,128)(2,1)} %get-tuple-element.264), kind=kOutput, calls=%fused_computation.26.clone.1 | convolution fusion | flops 1610612736 | bytes 7340032 | tf_op jit(solution)/shard_map/while/body/eval_jaxpr/dot_general | solution.py:28
  51.3 1.0 constant_dynamic-update-slice_fusion.4
  52.3 6.5 %copy.12 = bf16[2,512,8,256]{3,1,0,2:T(8,128)(2,1)} copy(bf16[2,512,8,256]{1,3,2,0:T(8,128)(2,1)} %bitcast.65) | data formatting | bytes 8388608 | tf_op jit(solution)/shard_map/reshape | solution.py:78
  58.8 5.6 %all-to-all-start = ((bf16[2,512,8,256]{3,1,0,2:T(8,128)(2,1)}), bf16[2,512,8,256]{3,1,0,2:T(8,128)(2,1)}, u32[]{:S(2)}, u32[]{:S(2)}) async-start(bf16[2,512,8,256]{3,1,0,2:T(8,128)(2,1)} %copy.12), calls=%async_computation | async-start | bytes 8388608 | tf_op jit(solution)/shard_map/all_to_all | solution.py:79
  64.5 1.3 dynamic_slice.22
  67.9 4.0 %reshape.43 = bf16[1049600]{0:T(1024)(128)(2,1)} reshape(bf16[2,512,1025]{2,1,0:T(8,128)(2,1)S(1)} %tile.20) | data formatting | bytes 4198400
  71.9 2.1 tile.21
  74.0 2.7 %slice.91 = bf16[2,524288]{1,0:T(2,128)(2,1)} slice(bf16[2,524800]{1,0:T(2,128)(2,1)S(1)} %tile.21), slice={[0:2], [0:524288]} | slice | bytes 4194304 | tf_op jit(solution)/shard_map/slice | solution.py:17
  76.7 3.6 %reshape.38 = bf16[1024,1024]{1,0:T(8,128)(2,1)S(1)} reshape(bf16[2,524288]{1,0:T(2,128)(2,1)} %slice.91) | data formatting | bytes 4194304 | tf_op jit(solution)/shard_map/reshape | solution.py:18
  80.3 29.7 %all-to-all-done = bf16[2,512,8,256]{3,1,0,2:T(8,128)(2,1)} async-done(((bf16[2,512,8,256]{3,1,0,2:T(8,128)(2,1)}), bf16[2,512,8,256]{3,1,0,2:T(8,128)(2,1)}, u32[]{:S(2)}, u32[]{:S(2)}) %all-to-all-start) | async-done | bytes 4194336 | tf_op jit(solution)/shard_map/all_to_all | solution.py:79
  110.0 2.5 %copy.13 = bf16[2,512,8,256]{3,1,2,0:T(8,128)(2,1)S(1)} copy(bf16[2,512,8,256]{3,1,0,2:T(8,128)(2,1)} %all-to-all-done) | data formatting | bytes 8388608 | tf_op jit(solution)/shard_map/all_to_all | solution.py:79
  112.4 2.4 %concatenate.14 = bf16[2,4608,256]{2,1,0:T(8,128)(2,1)} pad(bf16[2,4096,256]{2,1,0:T(8,128)(2,1)S(1)} %bitcast.66, bf16[]{:T(256)} %constant.87.clone.1), padding=0_0x0_512x0_0 | pad | bytes 8912898 | tf_op jit(solution)/shard_map/concatenate | solution.py:82
  114.9 4.5 %broadcast_in_dim.7.clone = bf16[2,4096,256]{2,0,1:T(2,128)(2,1)} broadcast(bf16[]{:T(256)} %constant.87.clone.1), dimensions={} | broadcast | bytes 4194306 | tf_op jit(solution)/shard_map/broadcast_in_dim | solution.py:45
  119.4 44.5 %while.27 = (s32[]{:T(128)}, bf16[2,4096,256]{2,0,1:T(2,128)(2,1)}, bf16[2,4608,256]{2,1,0:T(8,128)(2,1)}, bf16[1024,1024]{1,0:T(8,128)(2,1)S(1)}, s32[]{:T(128)...) while((s32[]{:T(128)}, bf16[2,4096,256]{2,0,1:T(2,128)(2,1)}, bf16[2,4608,256]{2,1,0:T(8,128)(2,1)}, ...), condition=%wide.region_3.4_spmd, body=%wide.region_2.3_spmd.sunk | while | flops 1074528256 | bytes 13107400 | solution.py:56
  119.4 1.8 convolution_bitcast_fusion.4
  121.2 1.8 convolution_bitcast_fusion.5
  123.8 1.2 constant_dynamic-update-slice_fusion.5
  125.0 1.8 convolution_bitcast_fusion.4
  126.8 1.8 convolution_bitcast_fusion.5
  129.4 1.2 constant_dynamic-update-slice_fusion.5
  130.5 1.8 convolution_bitcast_fusion.4
  132.3 1.8 convolution_bitcast_fusion.5
  134.9 1.2 constant_dynamic-update-slice_fusion.5
  136.1 1.8 convolution_bitcast_fusion.4
  137.9 1.8 convolution_bitcast_fusion.5
  140.5 1.2 constant_dynamic-update-slice_fusion.5
  141.6 1.8 convolution_bitcast_fusion.4
  143.4 1.8 convolution_bitcast_fusion.5
  146.0 1.2 constant_dynamic-update-slice_fusion.5
  147.2 1.8 convolution_bitcast_fusion.4
  149.0 1.8 convolution_bitcast_fusion.5
  151.6 1.2 constant_dynamic-update-slice_fusion.5
  152.8 1.8 convolution_bitcast_fusion.4
  154.6 1.8 convolution_bitcast_fusion.5
  157.2 1.2 constant_dynamic-update-slice_fusion.5
  158.3 1.8 convolution_bitcast_fusion.4
  160.1 1.8 convolution_bitcast_fusion.5
  162.7 1.2 constant_dynamic-update-slice_fusion.5
  163.9 55.1 %all_to_all.30 = bf16[2,4096,1,256]{3,0,2,1:T(2,128)(2,1)S(1)} all-to-all(bf16[2,4096,1,256]{3,0,2,1:T(2,128)(2,1)} %bitcast.64), channel_id=1, replica_groups=mesh['az'=8,'rg'=4] {'az'}, dimensions={1} | all-to-all | bytes 8388608 | tf_op jit(solution)/shard_map/all_to_all | solution.py:85
  219.0 4.4 %copy.15 = bf16[2,512,8,1,256]{4,2,1,0,3:T(8,128)(2,1)} copy(bf16[2,512,8,1,256]{4,0,1,2,3:T(2,128)(2,1)S(1)} %bitcast.67) | data formatting | bytes 8388608 | tf_op jit(solution)/shard_map/all_to_all | solution.py:85
  223.3 7.4 %reshape.40 = bf16[2,512,2048]{2,1,0:T(8,128)(2,1)} reshape(bf16[2,512,8,1,256]{4,2,1,0,3:T(8,128)(2,1)} %copy.15) | data formatting | bytes 8388608 | tf_op jit(solution)/shard_map/reshape | solution.py:86
  (41 shorter events, 9.4 us)
Async XLA Ops:
  0.0 67.7 %copy-start = (bf16[2,64,512]{2,1,0:T(8,128)(2,1)S(1)}, bf16[2,64,512]{2,1,0:T(8,128)(2,1)}, u32[]{:S(2)}) copy-start(bf16[2,64,512]{2,1,0:T(8,128)(2,1)} %param.10) | copy-start | bytes 393220
  1.9 16.0 %collective-permute-start = (bf16[2,512,256]{2,1,0:T(8,128)(2,1)}, bf16[2,512,256]{2,1,0:T(8,128)(2,1)}, u32[]{:S(2)}, u32[]{:S(2)}) collective-permute-start(bf16[2,512,256]{2,1,0:T(8,128)(2,1)} %slice.79), channel_id=1, source_target_pairs={{1,0},{2,1},{3,2},{5,4},{6,5},{7,6},{9,8},{10,9},{11,10},{13,12},{... | collective-permute-start | bytes 1572872 | tf_op jit(solution)/shard_map/ppermute | solution.py:10
  58.8 51.2 %all-to-all-start = ((bf16[2,512,8,256]{3,1,0,2:T(8,128)(2,1)}), bf16[2,512,8,256]{3,1,0,2:T(8,128)(2,1)}, u32[]{:S(2)}, u32[]{:S(2)}) async-start(bf16[2,512,8,256]{3,1,0,2:T(8,128)(2,1)} %copy.12), calls=%async_computation | async-start | bytes 8388608 | tf_op jit(solution)/shard_map/all_to_all | solution.py:79
where the time goes:
time: 234 us; the launch traced here: 231 us
  local copies, waits for them, and re-layouts  78.2 us (33%)
  blocking collectives  55.1 us (24%)
  matrix products  41.6 us (18%)
  waiting for transfers between devices  37.1 us (16%)
  other arithmetic  9.37 us (4%)
  starting transfers between devices  6.92 us (3%)
    all_to_all x1, blocking collectives, local(): lax.all_to_all(turned, 'az', split_axis=1, concat_axis=2, tiled=True)  55.1 us
    all_to_all x1, waiting for transfers between devices, local(): lax.all_to_all(grouped, 'az', split_axis=2, concat_axis=1, tiled=True)  29.7 us
    dot_general x8, matrix products, azimuth_one_block(): real_prod = jnp.dot(weights, segment[0], preferred_element_type=jnp.float32)  14.4 us
    dot_general x8, matrix products, azimuth_one_block(): imag_prod = jnp.dot(weights, segment[1], preferred_element_type=jnp.float32)  14.3 us
    dot_general x4, matrix products, range_one_block(): lax.dot_general(segment.reshape(2 * lines, span), weights, (((1,), (1,)),...  12.9 us
    dynamic_update_slice x16, local copies, waits for them, and re-layouts, azimuth_one_block(): lax.dynamic_update_slice_in_dim(current, piece, block_index * block_size,...  12.9 us
    ppermute x1, waiting for transfers between devices, passed_along(): return lax.ppermute(block, axis, route)  7.44 us
    reshape x1, local copies, waits for them, and re-layouts, local(): focused = returned.reshape(2, lines, columns)  7.37 us
  transfers between devices with their start and end apart: 2, of which 2 were waited for; matrix products, arithmetic and copies ran while one was open for 9% of the time, Pallas kernels for 0%

commit v1 on v0

v1 whole, which is shorter than its diff:
```python
import functools

import jax
import jax.numpy as jnp
from jax import lax
from jax.experimental import pallas as pl
from jax.experimental.pallas import tpu as pltpu
from jax.sharding import PartitionSpec as P

MESH = pl.DeviceIdType.MESH


def shifted_rows(row, rows, period):
    padded = jnp.concatenate(
        [row, jnp.zeros((1, period - row.shape[1]), row.dtype)], axis=1
    )
    spread = jnp.broadcast_to(padded, (rows, period))
    return pltpu.roll(spread, 0, 1, stride=1, stride_axis=0)


def kernel(
    az_size, rg_size, run, block,
    raw, chirp, az_ref, set_index, out,
    raw_v, comp, halo, res, range_w, az_w, az_f32,
    in_sem, out_sem, send_sem, recv_sem, edge_sem,
):
    taps = chirp.shape[1]
    az_taps = az_ref.shape[2]
    chunks, _, lines, width = comp.shape
    az, rg = lax.axis_index("az"), lax.axis_index("rg")

    barrier = pltpu.get_barrier_semaphore()
    for axis, me, size in (("az", az, az_size), ("rg", rg, rg_size)):
        for step in (1, size - 1):
            pl.semaphore_signal(
                barrier, inc=1, device_id={axis: lax.rem(me + step, size)},
                device_id_type=MESH,
            )

    def load(chunk):
        start = pl.multiple_of(chunk * width, width)
        return pltpu.make_async_copy(
            raw.at[:, :, pl.ds(start, width)], raw_v.at[chunk], in_sem.at[chunk]
        )

    def store(chunk):
        start = pl.multiple_of(chunk * width, width)
        return pltpu.make_async_copy(
            res.at[chunk], out.at[:, :, pl.ds(start, width)], out_sem.at[chunk]
        )

    def edge():
        return pltpu.make_async_remote_copy(
            src_ref=raw_v.at[0], dst_ref=raw_v.at[chunks],
            send_sem=edge_sem.at[0], recv_sem=edge_sem.at[1],
            device_id={"rg": lax.rem(rg + rg_size - 1, rg_size)}, device_id_type=MESH,
        )

    def send(chunk):
        return pltpu.make_async_remote_copy(
            src_ref=comp.at[chunk], dst_ref=halo.at[chunk],
            send_sem=send_sem.at[chunk], recv_sem=recv_sem.at[chunk],
            device_id={"az": lax.rem(az + az_size - 1, az_size)}, device_id_type=MESH,
        )

    for chunk in range(chunks):
        load(chunk).start()

    for part in range(2):
        row = chirp[pl.ds(part, 1), :].astype(jnp.float32)
        square = shifted_rows(row, width, width + taps)
        range_w[:, part * width:(part + 1) * width] = square.T.astype(jnp.bfloat16)

    az_f32[...] = az_ref[...].astype(jnp.float32)

    @pl.when(rg == rg_size - 1)
    def _():
        raw_v[chunks] = jnp.zeros((2, lines, width), jnp.bfloat16)

    @pl.when(az == az_size - 1)
    def _():
        def clear(chunk, carry):
            halo[chunk] = jnp.zeros((2, lines, width), jnp.bfloat16)
            return carry
        lax.fori_loop(0, chunks, clear, 0)

    load(0).wait()
    pl.semaphore_wait(barrier, 4)

    @pl.when(rg > 0)
    def _():
        edge().start()

    def range_chunk(chunk):
        for first in range(0, lines, block):
            rows = slice(first, first + block)
            real, imag = [
                jnp.dot(raw_v[chunk, part, rows, :], range_w[:width, :],
                        preferred_element_type=jnp.float32)
                + jnp.dot(raw_v[chunk + 1, part, rows, :], range_w[width:, :],
                          preferred_element_type=jnp.float32)
                for part in range(2)
            ]
            comp[chunk, 0, rows, :] = (real[:, :width] + imag[:, width:]).astype(jnp.bfloat16)
            comp[chunk, 1, rows, :] = (imag[:, :width] - real[:, width:]).astype(jnp.bfloat16)

        @pl.when(az > 0)
        def _():
            send(chunk).start()

    def early(chunk, carry):
        load(chunk + 1).wait()
        range_chunk(chunk)
        return carry

    lax.fori_loop(0, chunks - 1, early, 0)

    @pl.when(rg < rg_size - 1)
    def _():
        edge().wait_recv()

    range_chunk(chunks - 1)

    def focus(chunk, carry):
        @pl.when(az < az_size - 1)
        def _():
            send(chunk).wait_recv()

        for first_col in range(0, width, run):
            cols = slice(first_col, first_col + run)
            chosen = set_index[chunk * width + first_col]
            for part in range(2):
                row = az_f32[part, pl.ds(chosen, 1), :]
                square = shifted_rows(row, block, az_taps + 2 * block)
                az_w[part * block:(part + 1) * block, :] = (
                    square[:, :az_taps + block].astype(jnp.bfloat16)
                )
            for first in range(0, lines, block):
                own = min(lines - first, az_taps + block)
                rest = az_taps + block - own
                real, imag = [
                    jnp.dot(az_w[:, :own], comp[chunk, part, first:first + own, cols],
                            preferred_element_type=jnp.float32)
                    + jnp.dot(az_w[:, own:], halo[chunk, part, :rest, cols],
                              preferred_element_type=jnp.float32)
                    for part in range(2)
                ]
                rows = slice(first, first + block)
                res[chunk, 0, rows, cols] = (real[:block] + imag[block:]).astype(jnp.bfloat16)
                res[chunk, 1, rows, cols] = (imag[:block] - real[block:]).astype(jnp.bfloat16)
        store(chunk).start()
        return carry

    lax.fori_loop(0, chunks, focus, 0)

    @pl.when(rg > 0)
    def _():
        edge().wait_send()

    def finish(chunk, carry):
        @pl.when(az > 0)
        def _():
            send(chunk).wait_send()
        store(chunk).wait()
        return carry

    lax.fori_loop(0, chunks, finish, 0)


def local(az_size, rg_size, raw, chirp, az_ref, set_index):
    _, lines, columns = raw.shape
    taps = chirp.shape[1]
    az_taps = az_ref.shape[2]
    width = taps
    chunks = columns // width
    run = min(columns // az_size, width)
    block = az_taps // 2
    assert columns % width == 0 and width % run == 0
    assert lines >= az_taps and lines % block == 0
    halo_shape = (chunks, 2, lines, width)
    return pl.pallas_call(
        functools.partial(kernel, az_size, rg_size, run, block),
        out_shape=jax.ShapeDtypeStruct(raw.shape, jnp.bfloat16),
        in_specs=[
            pl.BlockSpec(memory_space=pl.ANY),
            pl.BlockSpec(memory_space=pltpu.VMEM),
            pl.BlockSpec(memory_space=pltpu.VMEM),
            pl.BlockSpec(memory_space=pltpu.SMEM),
        ],
        out_specs=pl.BlockSpec(memory_space=pl.ANY),
        scratch_shapes=[
            pltpu.VMEM((chunks + 1, 2, lines, width), jnp.bfloat16),
            pltpu.VMEM(halo_shape, jnp.bfloat16),
            pltpu.VMEM(halo_shape, jnp.bfloat16),
            pltpu.VMEM(halo_shape, jnp.bfloat16),
            pltpu.VMEM((width + taps, 2 * width), jnp.bfloat16),
            pltpu.VMEM((2 * block, az_taps + block), jnp.bfloat16),
            pltpu.VMEM(az_ref.shape, jnp.float32),
            pltpu.SemaphoreType.DMA((chunks,)),
            pltpu.SemaphoreType.DMA((chunks,)),
            pltpu.SemaphoreType.DMA((chunks,)),
            pltpu.SemaphoreType.DMA((chunks,)),
            pltpu.SemaphoreType.DMA((2,)),
        ],
        compiler_params=pltpu.CompilerParams(
            collective_id=0, has_side_effects=True, vmem_limit_bytes=40 * 2**20
        ),
        cost_estimate=pl.CostEstimate(
            flops=11 * 10**9, bytes_accessed=4 * raw.size, transcendentals=0
        ),
    )(raw, chirp, az_ref, set_index)


def solution(mesh):
    in_specs = (P(None, "az", "rg"), P(), P(), P("rg"))
    out_specs = P(None, "az", "rg")
    body = functools.partial(local, mesh.shape["az"], mesh.shape["rg"])
    return jax.shard_map(body, mesh=mesh, in_specs=in_specs, out_specs=out_specs, check_vma=False)
```

time: 234 us -> 62 us (0.26); the launches traced: 231 us -> 61.8 us
  local copies, waits for them, and re-layouts: 78.2 us -> 6.48 us
  Pallas kernels: 0 us -> 55.3 us
  blocking collectives: 55.1 us -> 0 us
  matrix products: 41.6 us -> 0 us
  waiting for transfers between devices: 37.1 us -> 0 us
  other arithmetic: 9.37 us -> 0 us
  starting transfers between devices: 6.92 us -> 0 us
    pallas_call x0 -> x1, Pallas kernels: none -> 55.3 us  [local(): pl.pallas_call(functools.partial(kernel, az_size, rg_size, run, block), o...]
    all_to_all x1 -> x0, blocking collectives: 55.1 us -> none  [local(): lax.all_to_all(turned, 'az', split_axis=1, concat_axis=2, tiled=True)]
    dot_general x20 -> x0, matrix products: 41.6 us -> none  [the longest x8 14.4 us: azimuth_one_block(): real_prod = jnp.dot(weights, segment[0], preferred_element_type=jnp.float32)]
    all_to_all x1 -> x0, waiting for transfers between devices: 29.7 us -> none  [local(): lax.all_to_all(grouped, 'az', split_axis=2, concat_axis=1, tiled=True)]
    reshape x4 -> x0, local copies, waits for them, and re-layouts: 19.6 us -> none  [the longest x1 7.37 us: local(): focused = returned.reshape(2, lines, columns)]
    dynamic_update_slice x24 -> x0, local copies, waits for them, and re-layouts: 19.2 us -> none  [the longest x16 12.9 us: azimuth_one_block(): lax.dynamic_update_slice_in_dim(current, piece, block_index * block_size,...]
    ppermute x1 -> x0, waiting for transfers between devices: 7.44 us -> none  [passed_along(): return lax.ppermute(block, axis, route)]
    dynamic_slice x6 -> x0, local copies, waits for them, and re-layouts: 7.32 us -> none  [the longest x4 6.04 us: range_one_block(): lax.dynamic_slice_in_dim(window, block_index * block_size, span, axis=2)]
  transfers between devices with their start and end apart: 2 -> 0, of which waited for: 2 -> 0; matrix products, arithmetic and copies ran while one was open for 9% -> 0% of each run, Pallas kernels for 0% -> 0%
where the time goes in v1:
time: 62 us; the launch traced here: 61.8 us
  Pallas kernels  55.3 us (89%)
  local copies, waits for them, and re-layouts  6.48 us (10%)
    pallas_call x1, Pallas kernels, local(): pl.pallas_call(functools.partial(kernel, az_size, rg_size, run, block), o...  55.3 us
    unnamed x9, local copies, waits for them, and re-layouts  6.48 us

profile of v1, /device:TPU:1, one launch (start us, length us, event | category | flops | bytes accessed | tf_op | source)
XLA Modules:
  0.0 61.8 jit_solution(1119470524519550986)
XLA Ops:
  0.0 0.0 copy-start
  0.0 2.2 %copy-done = bf16[2,512,2048]{2,1,0:T(8,128)(2,1)S(1)} copy-done((bf16[2,512,2048]{2,1,0:T(8,128)(2,1)S(1)}, bf16[2,512,2048]{2,1,0:T(8,128)(2,1)}, u32[]{:S(2)}) %copy-start) | copy-done | bytes 4194328
  2.2 0.0 copy-start.1
  2.2 0.9 %copy-done.1 = bf16[2,64,512]{2,1,0:T(8,128)(2,1)S(1)} copy-done((bf16[2,64,512]{2,1,0:T(8,128)(2,1)S(1)}, bf16[2,64,512]{2,1,0:T(8,128)(2,1)}, u32[]{:S(2)}) %copy-start.1) | copy-done | bytes 131096
  3.1 0.0 copy-start.2
  3.1 0.7 %copy-done.2 = s32[2048]{0:T(1024)S(1)} copy-done((s32[2048]{0:T(1024)S(1)}, s32[2048]{0:T(1024)}, u32[]{:S(2)}) %copy-start.2) | copy-done | bytes 8216
  3.8 0.0 copy-start.3
  3.8 0.7 %copy-done.3 = bf16[2,256]{1,0:T(2,128)(2,1)S(1)} copy-done((bf16[2,256]{1,0:T(2,128)(2,1)S(1)}, bf16[2,256]{1,0:T(2,128)(2,1)}, u32[]{:S(2)}) %copy-start.3) | copy-done | bytes 1048
  4.5 55.3 %shard_map.46 = bf16[2,512,2048]{2,1,0:T(8,128)(2,1)S(1)} custom-call(bf16[2,512,2048]{2,1,0:T(8,128)(2,1)S(1)} %copy-done, bf16[2,256]{1,0:T(2,128)(2,1)S(1)} %copy-done.3, bf16[2,64,512]{2,1,0:T(8,128)(2,1)S(1)} %copy-done.1, s32[2048]{0:T(1024)S(1)} %copy-done.2), custom_call_target="tpu_custom_call" | custom-call | flops 11000000512 | bytes 8388608 | tf_op jit(solution)/shard_map/pallas_call | solution.py:181
  59.7 2.0 %copy.6 = bf16[2,512,2048]{2,1,0:T(8,128)(2,1)} copy(bf16[2,512,2048]{2,1,0:T(8,128)(2,1)S(1)} %shard_map.46) | data formatting | bytes 8388608
Async XLA Ops:
  0.0 2.2 %copy-start = (bf16[2,512,2048]{2,1,0:T(8,128)(2,1)S(1)}, bf16[2,512,2048]{2,1,0:T(8,128)(2,1)}, u32[]{:S(2)}) copy-start(bf16[2,512,2048]{2,1,0:T(8,128)(2,1)} %raw.1) | copy-start | bytes 12582916
  2.2 0.9 %copy-start.1 = (bf16[2,64,512]{2,1,0:T(8,128)(2,1)S(1)}, bf16[2,64,512]{2,1,0:T(8,128)(2,1)}, u32[]{:S(2)}) copy-start(bf16[2,64,512]{2,1,0:T(8,128)(2,1)} %az_ref.1) | copy-start | bytes 393220
  3.1 0.7 %copy-start.2 = (s32[2048]{0:T(1024)S(1)}, s32[2048]{0:T(1024)}, u32[]{:S(2)}) copy-start(s32[2048]{0:T(1024)} %set_index.1) | copy-start | bytes 24580
  3.8 0.7 %copy-start.3 = (bf16[2,256]{1,0:T(2,128)(2,1)S(1)}, bf16[2,256]{1,0:T(2,128)(2,1)}, u32[]{:S(2)}) copy-start(bf16[2,256]{1,0:T(2,128)(2,1)} %chirp.1) | copy-start | bytes 3076

commit v2 on v1

v2 whole, which is shorter than its diff:
```python
import functools

import jax
import jax.numpy as jnp
from jax import lax
from jax.experimental import pallas as pl
from jax.experimental.pallas import tpu as pltpu
from jax.sharding import PartitionSpec as P

MESH = pl.DeviceIdType.MESH


def shifted_rows(row, rows, period):
    padded = jnp.concatenate(
        [row, jnp.zeros((1, period - row.shape[1]), row.dtype)], axis=1
    )
    spread = jnp.broadcast_to(padded, (rows, period))
    return pltpu.roll(spread, 0, 1, stride=1, stride_axis=0)


def kernel(
    az_size, rg_size, run,
    raw, chirp, az_ref, set_index, out,
    raw_v, comp, halo, res, range_w, az_w, sums, chirp_v, az_v, az_f32, sets,
    in_sem, out_sem, send_sem, recv_sem, edge_sem, small_sem,
):
    taps = chirp.shape[1]
    chunks, own_blocks, _, block, width = comp.shape
    halo_blocks = halo.shape[1]
    az, rg = lax.axis_index("az"), lax.axis_index("rg")

    barrier = pltpu.get_barrier_semaphore()
    for axis, me, size in (("az", az, az_size), ("rg", rg, rg_size)):
        for step in (1, size - 1):
            pl.semaphore_signal(
                barrier, inc=1, device_id={axis: lax.rem(me + step, size)},
                device_id_type=MESH,
            )

    def load(chunk):
        start = pl.multiple_of(chunk * width, width)
        return pltpu.make_async_copy(
            raw.at[:, :, pl.ds(start, width)], raw_v.at[chunk], in_sem.at[chunk]
        )

    def store(chunk, part):
        start = pl.multiple_of(chunk * width, width)
        return pltpu.make_async_copy(
            res.at[chunk, part],
            out.at[:, part * block:(part + 1) * block, pl.ds(start, width)],
            out_sem.at[chunk, part],
        )

    def edge():
        return pltpu.make_async_remote_copy(
            src_ref=raw_v.at[0], dst_ref=raw_v.at[chunks],
            send_sem=edge_sem.at[0], recv_sem=edge_sem.at[1],
            device_id={"rg": lax.rem(rg + rg_size - 1, rg_size)}, device_id_type=MESH,
        )

    def send(chunk, part):
        return pltpu.make_async_remote_copy(
            src_ref=comp.at[chunk, part], dst_ref=halo.at[chunk, part],
            send_sem=send_sem.at[chunk, part], recv_sem=recv_sem.at[chunk, part],
            device_id={"az": lax.rem(az + az_size - 1, az_size)}, device_id_type=MESH,
        )

    chirp_load = pltpu.make_async_copy(chirp, chirp_v, small_sem.at[0])
    az_load = pltpu.make_async_copy(az_ref, az_v, small_sem.at[1])
    sets_load = pltpu.make_async_copy(set_index, sets, small_sem.at[2])
    chirp_load.start()
    for chunk in range(chunks):
        load(chunk).start()
    az_load.start()
    sets_load.start()

    chirp_load.wait()
    for part in range(2):
        row = chirp_v[pl.ds(part, 1), :].astype(jnp.float32)
        square = shifted_rows(row, width, width + taps)
        range_w[:, part * width:(part + 1) * width] = square.T.astype(jnp.bfloat16)

    load(0).wait()
    pl.semaphore_wait(barrier, 4)

    @pl.when(rg > 0)
    def _():
        edge().start()

    @pl.when(rg == rg_size - 1)
    def _():
        raw_v[chunks] = jnp.zeros(raw_v.shape[1:], jnp.bfloat16)

    def range_chunk(chunk):
        for part in range(own_blocks):
            rows = slice(part * block, (part + 1) * block)
            real, imag = [
                jnp.dot(raw_v[chunk, side, rows, :], range_w[:width, :],
                        preferred_element_type=jnp.float32)
                + jnp.dot(raw_v[chunk + 1, side, rows, :], range_w[width:, :],
                          preferred_element_type=jnp.float32)
                for side in range(2)
            ]
            comp[chunk, part, 0] = (real[:, :width] + imag[:, width:]).astype(jnp.bfloat16)
            comp[chunk, part, 1] = (imag[:, :width] - real[:, width:]).astype(jnp.bfloat16)

            if part < halo_blocks:
                @pl.when(az > 0)
                def _():
                    send(chunk, part).start()

    def early(chunk, carry):
        load(chunk + 1).wait()
        range_chunk(chunk)
        return carry

    lax.fori_loop(0, chunks - 1, early, 0)

    az_load.wait()
    sets_load.wait()
    az_f32[...] = az_v[...].astype(jnp.float32)

    @pl.when(az == az_size - 1)
    def _():
        def clear(chunk, carry):
            halo[chunk] = jnp.zeros(halo.shape[1:], jnp.bfloat16)
            return carry
        lax.fori_loop(0, chunks, clear, 0)

    @pl.when(rg < rg_size - 1)
    def _():
        edge().wait_recv()

    range_chunk(chunks - 1)

    def product(first_col, shift, values):
        return jnp.dot(
            az_w[first_col // run, :, shift * block:(shift + 1) * block], values,
            preferred_element_type=jnp.float32,
        )

    def focus(chunk, carry):
        for first_col in range(0, width, run):
            cols = slice(first_col, first_col + run)
            chosen = sets[chunk * width + first_col]
            for side in range(2):
                row = az_f32[side, pl.ds(chosen, 1), :]
                square = shifted_rows(row, block, (halo_blocks + 2) * block)
                az_w[first_col // run, side * block:(side + 1) * block, :] = (
                    square[:, :(halo_blocks + 1) * block].astype(jnp.bfloat16)
                )
            for part in range(own_blocks):
                for side in range(2):
                    sums[part, side, :, cols] = sum(
                        product(first_col, shift, comp[chunk, part + shift, side, :, cols])
                        for shift in range(min(halo_blocks + 1, own_blocks - part))
                    )

        for landed in range(-1, halo_blocks):
            if landed >= 0:
                @pl.when(az < az_size - 1)
                def _():
                    send(chunk, landed).wait_recv()

            for part in range(own_blocks):
                shift = own_blocks + landed - part
                last = shift == halo_blocks
                if landed < 0 and not last or shift > halo_blocks:
                    continue
                for first_col in range(0, width, run):
                    cols = slice(first_col, first_col + run)
                    total = [
                        sums[part, side, :, cols]
                        if landed < 0
                        else sums[part, side, :, cols]
                        + product(first_col, shift, halo[chunk, landed, side, :, cols])
                        for side in range(2)
                    ]
                    if last:
                        real, imag = total
                        res[chunk, part, 0, :, cols] = (
                            real[:block] + imag[block:]
                        ).astype(jnp.bfloat16)
                        res[chunk, part, 1, :, cols] = (
                            imag[:block] - real[block:]
                        ).astype(jnp.bfloat16)
                    else:
                        for side in range(2):
                            sums[part, side, :, cols] = total[side]
                if last:
                    store(chunk, part).start()
        return carry

    lax.fori_loop(0, chunks, focus, 0)

    @pl.when(rg > 0)
    def _():
        edge().wait_send()

    def finish(chunk, carry):
        for part in range(halo_blocks):
            @pl.when(az > 0)
            def _():
                send(chunk, part).wait_send()

        for part in range(own_blocks):
            store(chunk, part).wait()
        return carry

    lax.fori_loop(0, chunks, finish, 0)


def local(az_size, rg_size, raw, chirp, az_ref, set_index):
    _, lines, columns = raw.shape
    taps = chirp.shape[1]
    az_taps = az_ref.shape[2]
    width = taps
    chunks = columns // width
    run = min(columns // az_size, width)
    block = az_taps // 2
    own_blocks, halo_blocks = lines // block, az_taps // block
    assert columns % width == 0 and width % run == 0
    assert lines % block == 0 and own_blocks == halo_blocks
    tile = (2, block, width)
    return pl.pallas_call(
        functools.partial(kernel, az_size, rg_size, run),
        out_shape=jax.ShapeDtypeStruct(raw.shape, jnp.bfloat16),
        in_specs=[pl.BlockSpec(memory_space=pltpu.HBM)] * 4,
        out_specs=pl.BlockSpec(memory_space=pl.ANY),
        scratch_shapes=[
            pltpu.VMEM((chunks + 1, 2, lines, width), jnp.bfloat16),
            pltpu.VMEM((chunks, own_blocks) + tile, jnp.bfloat16),
            pltpu.VMEM((chunks, halo_blocks) + tile, jnp.bfloat16),
            pltpu.VMEM((chunks, own_blocks) + tile, jnp.bfloat16),
            pltpu.VMEM((width + taps, 2 * width), jnp.bfloat16),
            pltpu.VMEM((width // run, 2 * block, (halo_blocks + 1) * block), jnp.bfloat16),
            pltpu.VMEM((own_blocks, 2, 2 * block, width), jnp.float32),
            pltpu.VMEM(chirp.shape, chirp.dtype),
            pltpu.VMEM(az_ref.shape, az_ref.dtype),
            pltpu.VMEM(az_ref.shape, jnp.float32),
            pltpu.SMEM(set_index.shape, set_index.dtype),
            pltpu.SemaphoreType.DMA((chunks,)),
            pltpu.SemaphoreType.DMA((chunks, own_blocks)),
            pltpu.SemaphoreType.DMA((chunks, halo_blocks)),
            pltpu.SemaphoreType.DMA((chunks, halo_blocks)),
            pltpu.SemaphoreType.DMA((2,)),
            pltpu.SemaphoreType.DMA((3,)),
        ],
        compiler_params=pltpu.CompilerParams(
            collective_id=0, has_side_effects=True, vmem_limit_bytes=60 * 2**20
        ),
        cost_estimate=pl.CostEstimate(
            flops=11 * 10**9, bytes_accessed=4 * raw.size, transcendentals=0
        ),
    )(raw, chirp, az_ref, set_index)


def solution(mesh):
    in_specs = (P(None, "az", "rg"), P(), P(), P("rg"))
    out_specs = P(None, "az", "rg")
    body = functools.partial(local, mesh.shape["az"], mesh.shape["rg"])
    return jax.shard_map(body, mesh=mesh, in_specs=in_specs, out_specs=out_specs, check_vma=False)
```

time: 62 us -> 59.6 us (0.961)
  local copies, waits for them, and re-layouts: 6.48 us -> 4.79 us
  Pallas kernels: 55.3 us -> 54.6 us
    unnamed x9 -> x1, local copies, waits for them, and re-layouts: 6.48 us -> 4.79 us
where the time goes in v2:
time: 59.6 us; the launch traced here: 59.4 us
  Pallas kernels  54.6 us (92%)
  local copies, waits for them, and re-layouts  4.79 us (8%)
    pallas_call x1, Pallas kernels, local(): pl.pallas_call(functools.partial(kernel, az_size, rg_size, run), out_shap...  54.6 us
    unnamed x1, local copies, waits for them, and re-layouts  4.79 us

profile of v2, /device:TPU:1, one launch (start us, length us, event | category | flops | bytes accessed | tf_op | source)
XLA Modules:
  0.0 59.4 jit_solution(15429876478897622178)
XLA Ops:
  0.0 54.6 %shard_map.46 = bf16[2,512,2048]{2,1,0:T(8,128)(2,1)} custom-call(bf16[2,512,2048]{2,1,0:T(8,128)(2,1)} %raw.1, bf16[2,256]{1,0:T(2,128)(2,1)} %chirp.1, bf16[2,64,512]{2,1,0:T(8,128)(2,1)} %az_ref.1, s32[2048]{0:T(1024)} %set_index.1), custom_call_target="tpu_custom_call" | custom-call | flops 11000000512 | bytes 8388608 | tf_op jit(solution)/shard_map/pallas_call | solution.py:225
  54.7 4.8 %copy.6 = bf16[2,512,2048]{2,1,0:T(8,128)(2,1)} copy(bf16[2,512,2048]{2,1,0:T(8,128)(2,1)} %shard_map.46) | data formatting | bytes 8388608

commit v3 on v2

--- a/solution.py
+++ b/solution.py
@@ -21,8 +21,8 @@
 def kernel(
     az_size, rg_size, run,
     raw, chirp, az_ref, set_index, out,
-    raw_v, comp, halo, res, range_w, az_w, sums, chirp_v, az_v, az_f32, sets,
-    in_sem, out_sem, send_sem, recv_sem, edge_sem, small_sem,
+    raw_v, comp, halo, range_w, az_w, sums, chirp_v, az_v, az_f32, sets,
+    in_sem, send_sem, recv_sem, edge_sem, small_sem,
 ):
     taps = chirp.shape[1]
     chunks, own_blocks, _, block, width = comp.shape
@@ -41,14 +41,6 @@
         start = pl.multiple_of(chunk * width, width)
         return pltpu.make_async_copy(
             raw.at[:, :, pl.ds(start, width)], raw_v.at[chunk], in_sem.at[chunk]
-        )
-
-    def store(chunk, part):
-        start = pl.multiple_of(chunk * width, width)
-        return pltpu.make_async_copy(
-            res.at[chunk, part],
-            out.at[:, part * block:(part + 1) * block, pl.ds(start, width)],
-            out_sem.at[chunk, part],
         )
 
     def edge():
@@ -178,17 +170,17 @@
                     ]
                     if last:
                         real, imag = total
-                        res[chunk, part, 0, :, cols] = (
+                        rows = slice(part * block, (part + 1) * block)
+                        start = pl.multiple_of(chunk * width + first_col, run)
+                        out[0, rows, pl.ds(start, run)] = (
                             real[:block] + imag[block:]
                         ).astype(jnp.bfloat16)
-                        res[chunk, part, 1, :, cols] = (
+                        out[1, rows, pl.ds(start, run)] = (
                             imag[:block] - real[block:]
                         ).astype(jnp.bfloat16)
                     else:
                         for side in range(2):
                             sums[part, side, :, cols] = total[side]
-                if last:
-                    store(chunk, part).start()
         return carry
 
     lax.fori_loop(0, chunks, focus, 0)
@@ -202,9 +194,6 @@
             @pl.when(az > 0)
             def _():
                 send(chunk, part).wait_send()
-
-        for part in range(own_blocks):
-            store(chunk, part).wait()
         return carry
 
     lax.fori_loop(0, chunks, finish, 0)
@@ -224,14 +213,13 @@
     tile = (2, block, width)
     return pl.pallas_call(
         functools.partial(kernel, az_size, rg_size, run),
-        out_shape=jax.ShapeDtypeStruct(raw.shape, jnp.bfloat16),
-        in_specs=[pl.BlockSpec(memory_space=pltpu.HBM)] * 4,
-        out_specs=pl.BlockSpec(memory_space=pl.ANY),
+        out_shape=pltpu.VMEM(raw.shape, jnp.bfloat16),
+        in_specs=[pl.BlockSpec(memory_space=pl.ANY)] * 4,
+        out_specs=pl.BlockSpec(memory_space=pltpu.VMEM),
         scratch_shapes=[
             pltpu.VMEM((chunks + 1, 2, lines, width), jnp.bfloat16),
             pltpu.VMEM((chunks, own_blocks) + tile, jnp.bfloat16),
             pltpu.VMEM((chunks, halo_blocks) + tile, jnp.bfloat16),
-            pltpu.VMEM((chunks, own_blocks) + tile, jnp.bfloat16),
             pltpu.VMEM((width + taps, 2 * width), jnp.bfloat16),
             pltpu.VMEM((width // run, 2 * block, (halo_blocks + 1) * block), jnp.bfloat16),
             pltpu.VMEM((own_blocks, 2, 2 * block, width), jnp.float32),
@@ -240,14 +228,13 @@
             pltpu.VMEM(az_ref.shape, jnp.float32),
             pltpu.SMEM(set_index.shape, set_index.dtype),
             pltpu.SemaphoreType.DMA((chunks,)),
-            pltpu.SemaphoreType.DMA((chunks, own_blocks)),
             pltpu.SemaphoreType.DMA((chunks, halo_blocks)),
             pltpu.SemaphoreType.DMA((chunks, halo_blocks)),
             pltpu.SemaphoreType.DMA((2,)),
             pltpu.SemaphoreType.DMA((3,)),
         ],
         compiler_params=pltpu.CompilerParams(
-            collective_id=0, has_side_effects=True, vmem_limit_bytes=60 * 2**20
+            collective_id=0, has_side_effects=True, vmem_limit_bytes=56 * 2**20
         ),
         cost_estimate=pl.CostEstimate(
             flops=11 * 10**9, bytes_accessed=4 * raw.size, transcendentals=0

time: 59.6 us -> 56 us (0.940)
  local copies, waits for them, and re-layouts: 4.79 us -> 2.02 us
  Pallas kernels: 54.6 us -> 53.8 us
    unnamed x1, local copies, waits for them, and re-layouts: 4.79 us -> 2.02 us
    pallas_call x1, Pallas kernels: 54.6 us -> 53.8 us  [local(): pl.pallas_call(functools.partial(kernel, az_size, rg_size, run), out_shap...]
where the time goes in v3:
time: 56 us; the launch traced here: 55.8 us
  Pallas kernels  53.8 us (96%)
  local copies, waits for them, and re-layouts  2.02 us (4%)
    pallas_call x1, Pallas kernels, local(): pl.pallas_call(functools.partial(kernel, az_size, rg_size, run), out_shap...  53.8 us
    unnamed x1, local copies, waits for them, and re-layouts  2.02 us

profile of v3, /device:TPU:1, one launch (start us, length us, event | category | flops | bytes accessed | tf_op | source)
XLA Modules:
  0.0 55.8 jit_solution(16157192666567315116)
XLA Ops:
  0.0 53.8 %shard_map.46 = bf16[2,512,2048]{2,1,0:T(8,128)(2,1)S(1)} custom-call(bf16[2,512,2048]{2,1,0:T(8,128)(2,1)} %raw.1, bf16[2,256]{1,0:T(2,128)(2,1)} %chirp.1, bf16[2,64,512]{2,1,0:T(8,128)(2,1)} %az_ref.1, s32[2048]{0:T(1024)} %set_index.1), custom_call_target="tpu_custom_call" | custom-call | flops 11000000512 | bytes 8388608 | tf_op jit(solution)/shard_map/pallas_call | solution.py:214
  53.8 2.0 %copy.6 = bf16[2,512,2048]{2,1,0:T(8,128)(2,1)} copy(bf16[2,512,2048]{2,1,0:T(8,128)(2,1)S(1)} %shard_map.46) | data formatting | bytes 8388608

commit v4 on v3

--- a/solution.py
+++ b/solution.py
@@ -11,9 +11,11 @@
 
 
 def shifted_rows(row, rows, period):
-    padded = jnp.concatenate(
-        [row, jnp.zeros((1, period - row.shape[1]), row.dtype)], axis=1
-    )
+    padded = row
+    if row.shape[1] < period:
+        padded = jnp.concatenate(
+            [row, jnp.zeros((1, period - row.shape[1]), row.dtype)], axis=1
+        )
     spread = jnp.broadcast_to(padded, (rows, period))
     return pltpu.roll(spread, 0, 1, stride=1, stride_axis=0)
 
@@ -43,6 +45,10 @@
             raw.at[:, :, pl.ds(start, width)], raw_v.at[chunk], in_sem.at[chunk]
         )
 
+    def start_load(chunk, carry):
+        load(chunk).start()
+        return carry
+
     def edge():
         return pltpu.make_async_remote_copy(
             src_ref=raw_v.at[0], dst_ref=raw_v.at[chunks],
@@ -61,27 +67,31 @@
     az_load = pltpu.make_async_copy(az_ref, az_v, small_sem.at[1])
     sets_load = pltpu.make_async_copy(set_index, sets, small_sem.at[2])
     chirp_load.start()
-    for chunk in range(chunks):
-        load(chunk).start()
+    load(0).start()
+    load(1).start()
+
+    circle = width + taps
+    total = lax.broadcasted_iota(jnp.int32, (taps, circle), 0) + lax.broadcasted_iota(
+        jnp.int32, (taps, circle), 1
+    )
+    reverse = ((total == 0) | (total == circle)).astype(jnp.bfloat16)
+    chirp_load.wait()
+    reversed_rows = jnp.dot(chirp_v[...], reverse, preferred_element_type=jnp.float32)
+    for side in range(2):
+        weights = shifted_rows(reversed_rows[side:side + 1], taps, circle).astype(jnp.bfloat16)
+        cols = slice(side * width, (side + 1) * width)
+        range_w[:taps, cols] = weights[:, :width]
+        range_w[taps:, cols] = weights[:, width:]
+
+    load(0).wait()
+    pl.semaphore_wait(barrier, 4)
+    lax.fori_loop(2, chunks, start_load, 0)
     az_load.start()
     sets_load.start()
 
-    chirp_load.wait()
-    for part in range(2):
-        row = chirp_v[pl.ds(part, 1), :].astype(jnp.float32)
-        square = shifted_rows(row, width, width + taps)
-        range_w[:, part * width:(part + 1) * width] = square.T.astype(jnp.bfloat16)
-
-    load(0).wait()
-    pl.semaphore_wait(barrier, 4)
-
     @pl.when(rg > 0)
     def _():
         edge().start()
-
-    @pl.when(rg == rg_size - 1)
-    def _():
-        raw_v[chunks] = jnp.zeros(raw_v.shape[1:], jnp.bfloat16)
 
     def range_chunk(chunk):
         for part in range(own_blocks):
@@ -118,6 +128,10 @@
             halo[chunk] = jnp.zeros(halo.shape[1:], jnp.bfloat16)
             return carry
         lax.fori_loop(0, chunks, clear, 0)
+
+    @pl.when(rg == rg_size - 1)
+    def _():
+        raw_v[chunks] = jnp.zeros(raw_v.shape[1:], jnp.bfloat16)
 
     @pl.when(rg < rg_size - 1)
     def _():
@@ -208,7 +222,7 @@
     run = min(columns // az_size, width)
     block = az_taps // 2
     own_blocks, halo_blocks = lines // block, az_taps // block
-    assert columns % width == 0 and width % run == 0
+    assert columns % width == 0 and width % run == 0 and chunks > 1
     assert lines % block == 0 and own_blocks == halo_blocks
     tile = (2, block, width)
     return pl.pallas_call(

time: 56 us -> 56 us (level)
  no operation moved by 1% of the time
where the time goes in v4:
time: 56 us; the launch traced here: 55.9 us
  Pallas kernels  53.8 us (96%)
  local copies, waits for them, and re-layouts  2.02 us (4%)
    pallas_call x1, Pallas kernels, local(): pl.pallas_call(functools.partial(kernel, az_size, rg_size, run), out_shap...  53.8 us
    unnamed x1, local copies, waits for them, and re-layouts  2.02 us

profile of v4, /device:TPU:1, one launch (start us, length us, event | category | flops | bytes accessed | tf_op | source)
XLA Modules:
  0.0 55.9 jit_solution(6695393127360952596)
XLA Ops:
  0.0 53.8 %shard_map.46 = bf16[2,512,2048]{2,1,0:T(8,128)(2,1)S(1)} custom-call(bf16[2,512,2048]{2,1,0:T(8,128)(2,1)} %raw.1, bf16[2,256]{1,0:T(2,128)(2,1)} %chirp.1, bf16[2,64,512]{2,1,0:T(8,128)(2,1)} %az_ref.1, s32[2048]{0:T(1024)} %set_index.1), custom_call_target="tpu_custom_call" | custom-call | flops 11000000512 | bytes 8388608 | tf_op jit(solution)/shard_map/pallas_call | solution.py:228
  53.8 2.0 %copy.6 = bf16[2,512,2048]{2,1,0:T(8,128)(2,1)} copy(bf16[2,512,2048]{2,1,0:T(8,128)(2,1)S(1)} %shard_map.46) | data formatting | bytes 8388608

commit v5 on v4

--- a/solution.py
+++ b/solution.py
@@ -213,6 +213,24 @@
     lax.fori_loop(0, chunks, finish, 0)
 
 
+def write_out(focused, out, sem):
+    pieces = sem.shape[1]
+    size = focused.shape[1] // pieces
+    copies = [
+        pltpu.make_async_copy(
+            focused.at[side, piece * size:(piece + 1) * size],
+            out.at[side, piece * size:(piece + 1) * size],
+            sem.at[side, piece],
+        )
+        for side in range(2)
+        for piece in range(pieces)
+    ]
+    for copy in copies:
+        copy.start()
+    for copy in copies:
+        copy.wait()
+
+
 def local(az_size, rg_size, raw, chirp, az_ref, set_index):
     _, lines, columns = raw.shape
     taps = chirp.shape[1]
@@ -225,7 +243,7 @@
     assert columns % width == 0 and width % run == 0 and chunks > 1
     assert lines % block == 0 and own_blocks == halo_blocks
     tile = (2, block, width)
-    return pl.pallas_call(
+    focused = pl.pallas_call(
         functools.partial(kernel, az_size, rg_size, run),
         out_shape=pltpu.VMEM(raw.shape, jnp.bfloat16),
         in_specs=[pl.BlockSpec(memory_space=pl.ANY)] * 4,
@@ -254,6 +272,14 @@
             flops=11 * 10**9, bytes_accessed=4 * raw.size, transcendentals=0
         ),
     )(raw, chirp, az_ref, set_index)
+    return pl.pallas_call(
+        write_out,
+        out_shape=jax.ShapeDtypeStruct(raw.shape, jnp.bfloat16),
+        in_specs=[pl.BlockSpec(memory_space=pltpu.VMEM)],
+        out_specs=pl.BlockSpec(memory_space=pl.ANY),
+        scratch_shapes=[pltpu.SemaphoreType.DMA((2, lines // (block // 2)))],
+        compiler_params=pltpu.CompilerParams(vmem_limit_bytes=16 * 2**20),
+    )(focused)
 
 
 def solution(mesh):

time: 56 us -> 56.1 us (level)
  Pallas kernels: 53.8 us -> 55.9 us
  local copies, waits for them, and re-layouts: 2.02 us -> 0 us
    pallas_call x0 -> x1, Pallas kernels: none -> 2.07 us  [local(): pl.pallas_call(write_out, out_shape=jax.ShapeDtypeStruct(raw.shape, jnp.b...]
    unnamed x1 -> x0, local copies, waits for them, and re-layouts: 2.02 us -> none
where the time goes in v5:
time: 56.1 us; the launch traced here: 55.9 us
  Pallas kernels  55.9 us (100%)
    pallas_call x1, Pallas kernels, local(): pl.pallas_call(functools.partial(kernel, az_size, rg_size, run), out_shap...  53.8 us
    pallas_call x1, Pallas kernels, local(): pl.pallas_call(write_out, out_shape=jax.ShapeDtypeStruct(raw.shape, jnp.b...  2.07 us

profile of v5, /device:TPU:1, one launch (start us, length us, event | category | flops | bytes accessed | tf_op | source)
XLA Modules:
  0.0 55.9 jit_solution(10540414012084775572)
XLA Ops:
  0.0 53.8 %shard_map.46.focused = bf16[2,512,2048]{2,1,0:T(8,128)(2,1)S(1)} custom-call(bf16[2,512,2048]{2,1,0:T(8,128)(2,1)} %raw.1, bf16[2,256]{1,0:T(2,128)(2,1)} %chirp.1, bf16[2,64,512]{2,1,0:T(8,128)(2,1)} %az_ref.1, s32[2048]{0:T(1024)} %set_index.1), custom_call_target="tpu_custom_call" | custom-call | flops 11000000512 | bytes 8388608 | tf_op jit(solution)/shard_map/pallas_call | solution.py:246
  53.8 2.1 %shard_map.47 = bf16[2,512,2048]{2,1,0:T(8,128)(2,1)} custom-call(bf16[2,512,2048]{2,1,0:T(8,128)(2,1)S(1)} %shard_map.46.focused), custom_call_target="tpu_custom_call" | custom-call | tf_op jit(solution)/shard_map/pallas_call | solution.py:275
